TPU v7x, 32 devices: a whole 2x2x4 slice. The times are simulated.
32 devices in a mesh: groups: 2 (over y), row: 4 (over x, core), col: 4 (over z).
Axes of the slice: x: 2, y: 2, z: 4, core: 2. Of those that a mesh axis runs over, the one named last changes fastest.
Arguments:
- shear_stress: float32 [8192, 512], P(('groups', 'row', 'col')), parts along dimension 0, may hold values from -0.3 to 0.3
- slip_state: float32 [8192, 512], P(('groups', 'row', 'col')), parts along dimension 0, may hold values from -0.15 to 0.15
- friction_a: float32 [8192, 512], P(('groups', 'row', 'col')), parts along dimension 0, may hold values from 0.15 to 0.3
- friction_b: float32 [8192, 512], P(('groups', 'row', 'col')), parts along dimension 0, may hold values from 0.1 to 0.4
- kernel: bfloat16 [8192, 4096], P(('groups', 'row'), 'col'), parts along dimension 0
- left_factors: bfloat16 [32, 16, 32, 256], P(('groups', 'row'), 'col'), parts along dimension 0, may hold values from -0.25 to 0.25
- right_factors: bfloat16 [32, 16, 32, 256], P(('groups', 'row'), 'col'), parts along dimension 0, may hold values from -0.375 to 0.375
- admissible: int32 [32, 16], P(('groups', 'row'), 'col'), parts along dimension 0, may hold values from 0 to 1, as said below
- ranks: int32 [32, 16], P(('groups', 'row'), 'col'), parts along dimension 0, may hold values from 1 to 32
Outputs:
- new_stress: float32 [8192, 512], P(('groups', 'row', 'col')), parts along dimension 0
- new_state: float32 [8192, 512], P(('groups', 'row', 'col')), parts along dimension 0
- mean_rate: float32 [8192, 512], P(('groups', 'row', 'col')), parts along dimension 0
There are 2 independent parts, one for each index of `groups`. A program takes and returns all parts, laid end to end along the dimension named above; each array names one. Nothing has to cross between parts.
Inputs may be any that keep to these rules, and one draw needn't show every extreme that they name: `admissible`: the sub-block that couples each patch with itself is dense.
All inputs are finite; a program needn't handle non-finite values.
Results may differ from a plain program's by a relative error of at most 0.0055.
Values may be sent and summed in bfloat16 or wider, within the bound.
A program may use at most 64 MiB of HBM per device.

v0:
```python
import jax
import jax.numpy as jnp
from jax import lax
from jax.sharding import PartitionSpec as P

time_step = 0.005


def slip_speed(stress, state_now, friction_a):
    return 2.0 * jnp.sinh(stress / friction_a) * jnp.exp(-state_now / friction_a)


def per_device(
    shear_stress,
    slip_state,
    friction_a,
    friction_b,
    kernel,
    left_factors,
    right_factors,
    admissible,
    ranks,
):
    members = shear_stress.shape[1]
    block_rows = kernel.shape[0]
    sub_count = admissible.shape[0]
    sub_size = block_rows // sub_count
    near_flag = admissible == 0
    rank_index = lax.broadcasted_iota(jnp.int32, left_factors.shape[:3], 2)
    live_rank = ((rank_index < ranks[:, :, None]) & (admissible[:, :, None] == 1)).astype(
        jnp.float32
    )

    def far_part(gathered):
        slip_subs = gathered.reshape(sub_count, sub_size, members)
        coefficients = jnp.einsum(
            "ijrb,jbe->ijre", right_factors, slip_subs, preferred_element_type=jnp.float32
        )
        coefficients = (coefficients * live_rank[..., None]).astype(jnp.bfloat16)
        result = jnp.einsum(
            "ijrb,ijre->ibe", left_factors, coefficients, preferred_element_type=jnp.float32
        )
        return result.reshape(block_rows, members)

    blocks = kernel.reshape(sub_count, sub_size, sub_count, sub_size)
    zeroed = jnp.where(near_flag[:, None, :, None], blocks, jnp.zeros((), kernel.dtype))
    kernel_tile = zeroed.reshape(block_rows, block_rows)

    def friction_rates(stress, state_now):
        speed_now = slip_speed(stress, state_now, friction_a)
        deficit = (1.0 - speed_now).astype(jnp.bfloat16)
        gathered = lax.all_gather(deficit, "row", axis=0, tiled=True)
        partial_value = jnp.dot(
            kernel_tile, gathered, preferred_element_type=jnp.float32
        ) + far_part(gathered)
        stress_rate = lax.psum_scatter(
            partial_value.astype(jnp.bfloat16), "col", scatter_dimension=0, tiled=True
        ).astype(jnp.float32)
        state_rate = friction_b * (jnp.exp(-state_now / friction_b) - speed_now)
        return (stress_rate, state_rate)

    first_stress, first_state = friction_rates(shear_stress, slip_state)
    mid_stress = shear_stress + time_step * first_stress
    mid_state = slip_state + time_step * first_state
    second_stress, second_state = friction_rates(mid_stress, mid_state)
    mean_rate = 0.5 * (first_stress + second_stress)
    new_stress = shear_stress + time_step * mean_rate
    new_state = slip_state + 0.5 * time_step * (first_state + second_state)
    return (new_stress, new_state, mean_rate)


def solution(mesh):
    return jax.shard_map(
        per_device,
        mesh=mesh,
        in_specs=(
            P(("groups", "row", "col"), None),
            P(("groups", "row", "col"), None),
            P(("groups", "row", "col"), None),
            P(("groups", "row", "col"), None),
            P(("groups", "row"), "col"),
            P(("groups", "row"), "col", None, None),
            P(("groups", "row"), "col", None, None),
            P(("groups", "row"), "col"),
            P(("groups", "row"), "col"),
        ),
        out_specs=(
            P(("groups", "row", "col"), None),
            P(("groups", "row", "col"), None),
            P(("groups", "row", "col"), None),
        ),
        check_vma=False,
    )
```

profile of v0, /device:TPU:0, one launch (start us, length us, event | category | flops | bytes accessed | tf_op | source)
XLA Modules:
  0.0 125.2 jit_solution(13677343020455048079)
XLA Ops:
  7.2 0.0 copy-start
  7.2 0.0 all-gather.3.cloned.1.call-start
  7.2 2.8 %subtract_convert_fusion.1 = (bf16[256,512]{1,0:T(8,128)(2,1)}, f32[256,512]{1,0:T(8,128)}) fusion(f32[256,512]{1,0:T(8,128)} %param.11, f32[256,512]{1,0:T(8,128)} %param.10, f32[256,512]{1,0:T(8,128)} %param.9), kind=kLoop, calls=%fused_computation.35 | loop fusion | flops 2228224 | bytes 2359296 | tf_op jit(solution)/shard_map/convert_element_type | solution.py:51
  10.1 0.0 all-gather.3.cloned.1.call-update
  10.1 0.0 reduce-scatter.3.cloned.1.call-start
  10.1 0.6 broadcast_in_dim.19
  10.8 1.5 %copy.14 = pred[128,8,4,256]{3,1,2,0:T(8,128)(4,1)} copy(pred[128,8,4,256]{3,2,1,0:T(4,128)(4,1)S(1)} %bitcast.51) | data formatting | bytes 2097152
  12.3 0.1 fusion.22
  12.4 17.3 %all-gather.3.cloned.1.call-done = bf16[1024,512]{1,0:T(8,128)(2,1)} async-done(((bf16[256,512]{1,0:T(8,128)(2,1)}), bf16[1024,512]{1,0:T(8,128)(2,1)}) %all-gather.3.cloned.1.call-update) | async-done | bytes 1048592 | tf_op jit(solution)/shard_map/all_gather | solution.py:52
  29.7 1.9 %fusion.6 = f32[4,512,256,1]{1,2,3,0:T(8,128)S(1)} fusion(bf16[4,4,32,256]{3,2,1,0:T(8,128)(2,1)S(1)} %copy-done, bf16[4,256,512,1]{2,1,0,3:T(8,128)(2,1)} %bitcast.52, bf16[4,4,32,256]{3,2,1,0:T(8,128)(2,1)S(1)} %copy-done.3, f32[4,4,32]{2,1,0:T(4,128)S(1)} %fusion.22), kind=kOutput, calls=%fused_computation.10 | convolution fusion | flops 268959744 | bytes 3672064 | tf_op jit(solution)/shard_map/ijrb,ijre->ibe/dot_general | solution.py:40
  31.6 4.5 %fusion.1 = bf16[1024,512]{1,0:T(8,128)(2,1)} fusion(f32[4,512,256,1]{1,2,3,0:T(8,128)S(1)} %fusion.6, bf16[1024,512]{1,0:T(8,128)(2,1)} %all-gather.3.cloned.1.call-done, pred[1024,1024]{1,0:T(8,128)(4,1)} %bitcast.54, bf16[1024,1024]{1,0:T(8,128)(2,1)} %param.13), kind=kOutput, calls=%fused_computation.3 | convolution fusion | flops 1075838976 | bytes 7340032 | tf_op jit(solution)/shard_map/dot_general | solution.py:53
  36.1 0.0 reduce-scatter.3.cloned.1.call-update
  36.1 0.0 all-gather.5.cloned.1.call-start
  36.2 27.2 %reduce-scatter.3.cloned.1.call-done = bf16[256,512]{1,0:T(8,128)(2,1)} async-done(((bf16[1024,512]{1,0:T(8,128)(2,1)}), bf16[256,512]{1,0:T(8,128)(2,1)}) %reduce-scatter.3.cloned.1.call-update) | async-done | bytes 262160 | tf_op jit(solution)/shard_map/reduce_scatter | solution.py:56
  63.4 3.1 %multiply_add_fusion = (f32[256,512]{1,0:T(8,128)}, f32[256,512]{1,0:T(8,128)S(1)}) fusion(f32[256,512]{1,0:T(8,128)} %param.10, f32[256,512]{1,0:T(8,128)} %param.12, f32[256,512]{1,0:T(8,128)} %get-tuple-element.6, f32[256,512]{1,0:T(8,128)S(1)} %copy-done.2, f32[256,512]{1,0:T(8,128)S(1)} %copy-done.1, bf16[256,512]{1,0:T(8,128)(2,1)} %reduce-scatter.3.cloned.1.call-done), kind=kLoop, calls=%fused_computation.27 | loop fusion | flops 3932160 | bytes 3932160 | tf_op jit(solution)/shard_map/add | solution.py:68
  66.6 0.7 subtract_convert_fusion
  67.3 0.0 all-gather.5.cloned.1.call-update
  67.3 0.0 reduce-scatter.5.cloned.1.call-start
  67.4 15.5 %all-gather.5.cloned.1.call-done = bf16[1024,512]{1,0:T(8,128)(2,1)} async-done(((bf16[256,512]{1,0:T(8,128)(2,1)}), bf16[1024,512]{1,0:T(8,128)(2,1)}) %all-gather.5.cloned.1.call-update) | async-done | bytes 1048592 | tf_op jit(solution)/shard_map/all_gather | solution.py:52
  82.9 1.9 %fusion.7 = f32[4,512,256,1]{1,2,3,0:T(8,128)S(1)} fusion(bf16[4,4,32,256]{3,2,1,0:T(8,128)(2,1)S(1)} %copy-done, bf16[4,256,512,1]{2,1,0,3:T(8,128)(2,1)} %bitcast.53, bf16[4,4,32,256]{3,2,1,0:T(8,128)(2,1)S(1)} %copy-done.4, f32[4,4,32]{2,1,0:T(4,128)S(1)} %fusion.22), kind=kOutput, calls=%fused_computation.11 | convolution fusion | flops 268959744 | bytes 3672064 | tf_op jit(solution)/shard_map/ijrb,ijre->ibe/dot_general | solution.py:40
  84.8 4.5 %fusion = bf16[1024,512]{1,0:T(8,128)(2,1)} fusion(f32[4,512,256,1]{1,2,3,0:T(8,128)S(1)} %fusion.7, bf16[1024,512]{1,0:T(8,128)(2,1)} %all-gather.5.cloned.1.call-done, pred[1024,1024]{1,0:T(8,128)(4,1)} %bitcast.55, bf16[1024,1024]{1,0:T(8,128)(2,1)} %param.13), kind=kOutput, calls=%fused_computation.1 | convolution fusion | flops 1075838976 | bytes 7340032 | tf_op jit(solution)/shard_map/dot_general | solution.py:53
  89.3 0.0 reduce-scatter.5.cloned.1.call-update
  89.3 27.3 %reduce-scatter.5.cloned.1.call-done = bf16[256,512]{1,0:T(8,128)(2,1)} async-done(((bf16[1024,512]{1,0:T(8,128)(2,1)}), bf16[256,512]{1,0:T(8,128)(2,1)}) %reduce-scatter.5.cloned.1.call-update) | async-done | bytes 262160 | tf_op jit(solution)/shard_map/reduce_scatter | solution.py:56
  116.6 2.1 %fusion.20 = (f32[256,512]{1,0:T(8,128)}, f32[256,512]{1,0:T(8,128)}) fusion(bf16[256,512]{1,0:T(8,128)(2,1)} %reduce-scatter.5.cloned.1.call-done, bf16[256,512]{1,0:T(8,128)(2,1)S(1)} %copy-done.5, f32[256,512]{1,0:T(8,128)S(1)} %copy-done.1), kind=kLoop, calls=%fused_computation.37 | loop fusion | flops 786432 | bytes 2097152 | tf_op jit(solution)/shard_map/mul | solution.py:66
  (16 shorter events, 0.0 us)
Async XLA Ops:
  7.2 22.5 %copy-start = (bf16[4,4,32,256]{3,2,1,0:T(8,128)(2,1)S(1)}, bf16[4,4,32,256]{3,2,1,0:T(8,128)(2,1)}, u32[]{:S(2)}) copy-start(bf16[4,4,32,256]{3,2,1,0:T(8,128)(2,1)} %param.14) | copy-start | bytes 786436
  7.2 2.9 %copy-start.6 = (s32[4,4]{1,0:T(4,128)S(1)}, s32[4,4]{1,0:T(4,128)}, u32[]{:S(2)}) copy-start(s32[4,4]{1,0:T(4,128)} %param.16) | copy-start | bytes 196
  7.2 22.5 %all-gather.3.cloned.1.call-start = ((), (), s32[]{:S(2)}) async-start(), calls=%async_computation.2 | async-start | bytes 1310720 | tf_op jit(solution)/shard_map/all_gather | solution.py:52
  10.0 2.2 %copy-start.7 = (s32[4,4]{1,0:T(4,128)S(1)}, s32[4,4]{1,0:T(4,128)}, u32[]{:S(2)}) copy-start(s32[4,4]{1,0:T(4,128)} %param.17) | copy-start | bytes 196
  10.0 19.6 %copy-start.3 = (bf16[4,4,32,256]{3,2,1,0:T(8,128)(2,1)S(1)}, bf16[4,4,32,256]{3,2,1,0:T(8,128)(2,1)}, u32[]{:S(2)}) copy-start(bf16[4,4,32,256]{3,2,1,0:T(8,128)(2,1)} %param.15) | copy-start | bytes 786436
  10.1 53.3 %reduce-scatter.3.cloned.1.call-start = ((), (), s32[]{:S(2)}) async-start(), calls=%async_computation.3 | async-start | bytes 1310720 | tf_op jit(solution)/shard_map/reduce_scatter | solution.py:56
  31.6 31.8 %copy-start.1 = (f32[256,512]{1,0:T(8,128)S(1)}, f32[256,512]{1,0:T(8,128)}, u32[]{:S(2)}) copy-start(f32[256,512]{1,0:T(8,128)} %param.9) | copy-start | bytes 1572868
  31.6 31.8 %copy-start.2 = (f32[256,512]{1,0:T(8,128)S(1)}, f32[256,512]{1,0:T(8,128)}, u32[]{:S(2)}) copy-start(f32[256,512]{1,0:T(8,128)} %param.11) | copy-start | bytes 1572868
  36.1 46.8 %all-gather.5.cloned.1.call-start = ((), (), s32[]{:S(2)}) async-start(), calls=%async_computation.4 | async-start | bytes 1310720 | tf_op jit(solution)/shard_map/all_gather | solution.py:52
  63.4 19.4 %copy-start.4 = (bf16[4,4,32,256]{3,2,1,0:T(8,128)(2,1)S(1)}, bf16[4,4,32,256]{3,2,1,0:T(8,128)(2,1)}, u32[]{:S(2)}) copy-start(bf16[4,4,32,256]{3,2,1,0:T(8,128)(2,1)} %param.15) | copy-start | bytes 786436
  67.3 49.3 %reduce-scatter.5.cloned.1.call-start = ((), (), s32[]{:S(2)}) async-start(), calls=%async_computation.5 | async-start | bytes 1310720 | tf_op jit(solution)/shard_map/reduce_scatter | solution.py:56
  84.8 31.8 %copy-start.5 = (bf16[256,512]{1,0:T(8,128)(2,1)S(1)}, bf16[256,512]{1,0:T(8,128)(2,1)}, u32[]{:S(2)}) copy-start(bf16[256,512]{1,0:T(8,128)(2,1)} %reduce-scatter.3.cloned.1.call-done) | copy-start | bytes 786436
Sparse Core Ops, SparseCore 0:
  10.2 19.4 all-gather.2
  36.2 27.1 reduce-scatter.2
  67.4 15.3 all-gather.4
  89.4 27.1 reduce-scatter.4
where the time goes:
time: 125 us
  waiting for transfers between devices  87.4 us (70%)
  between operations  13.8 us (11%)
  matrix products  12.8 us (10%)
  other arithmetic  8.85 us (7%)
  local copies, waits for them, and re-layouts  2.16 us (2%)
    reduce_scatter x2, waiting for transfers between devices, friction_rates(): lax.psum_scatter(partial_value.astype(jnp.bfloat16), 'col', scatter_dimen...  54.5 us
    all_gather x2, waiting for transfers between devices, friction_rates(): gathered = lax.all_gather(deficit, 'row', axis=0, tiled=True)  32.8 us
    dot_general x2, matrix products, friction_rates(): jnp.dot(kernel_tile, gathered, preferred_element_type=jnp.float32)  8.94 us
    dot_general x2, matrix products, far_part(): jnp.einsum('ijrb,ijre->ibe', left_factors, coefficients, preferred_elemen...  3.84 us
    convert_element_type x2, other arithmetic, friction_rates(): deficit = (1.0 - speed_now).astype(jnp.bfloat16)  3.55 us
    add x1, other arithmetic, per_device(): new_state = slip_state + 0.5 * time_step * (first_state + second_state)  3.14 us
  transfers between devices with their start and end apart: 4, of which 4 were waited for; matrix products, arithmetic and copies ran while one was open for 2% of the time, Pallas kernels for 0%

commit v1 on v0

v1 whole, which is shorter than its diff:
```python
import functools

import jax
import jax.numpy as jnp
from jax import lax
from jax.experimental import pallas as pl
from jax.experimental.pallas import tpu as pltpu
from jax.sharding import PartitionSpec as P

time_step = 0.005
LANES = 128
LAG_FORWARD = 1
LAG_FINAL = 2
MESH = pl.DeviceIdType.MESH
F32 = jnp.float32
BF16 = jnp.bfloat16


def step_kernel(
    n_row,
    n_col,
    shear_hbm,
    slip_hbm,
    fa_hbm,
    fb_hbm,
    kernel_hbm,
    left_hbm,
    right_hbm,
    admissible,
    ranks,
    stress_hbm,
    state_hbm,
    mean_hbm,
    s0,
    v0,
    fa,
    fb,
    kern,
    left,
    right,
    dense,
    state_rate,
    first_stress,
    first_state,
    total,
    slip_all,
    part,
    from_low,
    from_high,
    out_stress,
    out_state,
    out_mean,
    in_sem,
    op_sem,
    out_sem,
    gather_send,
    gather_recv,
    up_send,
    up_recv,
    down_send,
    down_recv,
):
    row = lax.axis_index("row")
    col = lax.axis_index("col")
    chunks, q = s0.shape[0], s0.shape[1]
    steps = 2 * chunks
    subs = admissible.shape[0]
    sub = left.shape[3]
    rank_max = left.shape[2]
    lower_half = col < n_col // 2

    def load(which, e):
        src = (shear_hbm, slip_hbm, fa_hbm, fb_hbm)[which]
        dst = (s0, v0, fa, fb)[which]
        return pltpu.make_async_copy(
            src.at[:, pl.ds(e * LANES, LANES)], dst.at[e], in_sem.at[which, e]
        )

    def load_op(which):
        src = (kernel_hbm, left_hbm, right_hbm)[which]
        dst = (kern, left, right)[which]
        return pltpu.make_async_copy(src, dst, op_sem.at[which])

    barrier = pltpu.get_barrier_semaphore()
    for k in range(1, n_row):
        pl.semaphore_signal(
            barrier, inc=1, device_id={"row": lax.rem(row + k, n_row)}, device_id_type=MESH
        )

    @pl.when(col > 0)
    def _():
        pl.semaphore_signal(barrier, inc=1, device_id={"col": col - 1}, device_id_type=MESH)

    @pl.when(col < n_col - 1)
    def _():
        pl.semaphore_signal(barrier, inc=1, device_id={"col": col + 1}, device_id_type=MESH)

    for e in range(chunks):
        for which in range(4):
            load(which, e).start()
        if e == 0:
            for which in range(3):
                load_op(which).start()

    def deficit_step(sec, e, stress, state):
        a, b = fa[e], fb[e]
        inv_a = 1.0 / a
        speed = jnp.exp((stress - state) * inv_a) - jnp.exp((-stress - state) * inv_a)
        slip_all[sec, e, pl.ds(pl.multiple_of(row * q, q), q), :] = (1.0 - speed).astype(BF16)
        state_rate[sec, e] = b * (jnp.exp(-state / b) - speed)

    def gather_copy(sec, e, k):
        block = slip_all.at[sec, e, pl.ds(pl.multiple_of(row * q, q), q), :]
        return pltpu.make_async_remote_copy(
            src_ref=block,
            dst_ref=block,
            send_sem=gather_send.at[sec, e, k - 1],
            recv_sem=gather_recv.at[sec, e, k - 1],
            device_id={"row": lax.rem(row + k, n_row)},
            device_id_type=MESH,
        )

    def start_gather(sec, e):
        for k in range(1, n_row):
            gather_copy(sec, e, k).start()

    def up_copy(sec, e, d):
        return pltpu.make_async_remote_copy(
            src_ref=part.at[sec, e, d],
            dst_ref=from_low.at[sec, e, d],
            send_sem=up_send.at[sec, e, d],
            recv_sem=up_recv.at[sec, e, d],
            device_id={"col": col + 1},
            device_id_type=MESH,
        )

    def down_copy(sec, e, d):
        return pltpu.make_async_remote_copy(
            src_ref=part.at[sec, e, d],
            dst_ref=from_high.at[sec, e, d],
            send_sem=down_send.at[sec, e, d],
            recv_sem=down_recv.at[sec, e, d],
            device_id={"col": col - 1},
            device_id_type=MESH,
        )

    def target(i):
        return jnp.where(lower_half, n_col - 1 - i, i)

    for which in range(4):
        load(which, 0).wait()
    deficit_step(0, 0, s0[0], v0[0])

    below, above = jnp.minimum(col, 1), jnp.minimum(n_col - 1 - col, 1)
    pl.semaphore_wait(barrier, n_row - 1 + below + above)

    start_gather(0, 0)

    @pl.loop(1, chunks)
    def _(e):
        for which in range(4):
            load(which, e).wait()
        deficit_step(0, e, s0[e], v0[e])
        start_gather(0, e)

    for which in range(3):
        load_op(which).wait()

    rank_at = lax.broadcasted_iota(jnp.int32, (rank_max, sub), 0)
    lane_at = lax.broadcasted_iota(jnp.int32, (sub, sub), 1)

    @pl.loop(0, subs)
    def _(i):
        rows = pl.ds(pl.multiple_of(i * sub, sub), sub)
        for j in range(subs):
            far = admissible[i, j]
            live = rank_at < far * ranks[i, j]
            factor = jnp.where(live, left[i, j].astype(F32), 0.0).astype(BF16)
            low = lax.dot_general(
                factor, right[i, j], (((0,), (0,)), ((), ())), preferred_element_type=F32
            )
            near = jnp.where(
                lane_at >= far * sub, kern[rows, pl.ds(j * sub, sub)].astype(F32), low
            )
            dense[rows, pl.ds(j * sub, sub)] = near.astype(BF16)

    def multiply(sec, e):
        for k in range(1, n_row):
            gather_copy(sec, e, k).wait_recv()
        slips = slip_all[sec, e]

        @pl.loop(0, n_col)
        def _(i):
            d = target(i)
            rows = pl.ds(pl.multiple_of(d * q, q), q)
            part[sec, e, d] = jnp.dot(
                dense[rows, :], slips, preferred_element_type=F32
            ).astype(BF16)

            @pl.when((col == 0) & (d > 0))
            def _():
                up_copy(sec, e, d).start()

            @pl.when((col == n_col - 1) & (d < col))
            def _():
                down_copy(sec, e, d).start()

    def forward(sec, e):
        @pl.loop(0, n_col)
        def _(i):
            d = target(i)

            @pl.when((col > 0) & (d > col))
            def _():
                up_copy(sec, e, d).wait_recv()
                part[sec, e, d] = (
                    part[sec, e, d].astype(F32) + from_low[sec, e, d].astype(F32)
                ).astype(BF16)
                up_copy(sec, e, d).start()

            @pl.when((col < n_col - 1) & (d < col))
            def _():
                down_copy(sec, e, d).wait_recv()
                part[sec, e, d] = (
                    part[sec, e, d].astype(F32) + from_high[sec, e, d].astype(F32)
                ).astype(BF16)
                down_copy(sec, e, d).start()

    def store(which, e):
        src = (out_stress, out_state, out_mean)[which]
        dst = (stress_hbm, state_hbm, mean_hbm)[which]
        return pltpu.make_async_copy(
            src.at[e], dst.at[:, pl.ds(e * LANES, LANES)], out_sem.at[which, e]
        )

    def finish(sec, e):
        total[...] = part[sec, e, col].astype(F32)

        @pl.when(col > 0)
        def _():
            up_copy(sec, e, col).wait_recv()
            total[...] += from_low[sec, e, col].astype(F32)

        @pl.when(col < n_col - 1)
        def _():
            down_copy(sec, e, col).wait_recv()
            total[...] += from_high[sec, e, col].astype(F32)

        @pl.when(sec == 0)
        def _():
            rate = total[...]
            first_stress[e] = rate
            deficit_step(
                1, e, s0[e] + time_step * rate, v0[e] + time_step * state_rate[0, e]
            )
            start_gather(1, e)

        @pl.when(sec == 1)
        def _():
            mean = 0.5 * (first_stress[e] + total[...])
            out_mean[e] = mean
            out_stress[e] = s0[e] + time_step * mean
            out_state[e] = v0[e] + 0.5 * time_step * (state_rate[0, e] + state_rate[1, e])
            for which in range(3):
                store(which, e).start()

    @pl.loop(0, steps + LAG_FINAL)
    def _(t):
        @pl.when(t < steps)
        def _():
            multiply(t // chunks, lax.rem(t, chunks))

        u = t - LAG_FORWARD

        @pl.when((u >= 0) & (u < steps))
        def _():
            forward(u // chunks, lax.rem(u, chunks))

        w = t - LAG_FINAL

        @pl.when(w >= 0)
        def _():
            finish(w // chunks, lax.rem(w, chunks))

    @pl.loop(0, steps)
    def _(t):
        sec, e = t // chunks, lax.rem(t, chunks)
        for k in range(1, n_row):
            gather_copy(sec, e, k).wait_send()

        @pl.loop(0, n_col)
        def _(d):
            @pl.when(d > col)
            def _():
                up_copy(sec, e, d).wait_send()

            @pl.when(d < col)
            def _():
                down_copy(sec, e, d).wait_send()

    @pl.loop(0, chunks)
    def _(e):
        for which in range(3):
            store(which, e).wait()


def per_device(
    n_row,
    n_col,
    shear_stress,
    slip_state,
    friction_a,
    friction_b,
    kernel,
    left_factors,
    right_factors,
    admissible,
    ranks,
):
    q, members = shear_stress.shape
    block = kernel.shape[0]
    chunks = members // LANES
    field = pltpu.VMEM((chunks, q, LANES), F32)
    sem = pltpu.SemaphoreType.DMA
    anywhere = pl.BlockSpec(memory_space=pl.ANY)
    scalars = pl.BlockSpec(memory_space=pltpu.SMEM)
    out = jax.ShapeDtypeStruct((q, members), F32)
    return tuple(
        pl.pallas_call(
            functools.partial(step_kernel, n_row, n_col),
            out_shape=(out, out, out),
            in_specs=[anywhere] * 7 + [scalars] * 2,
            out_specs=(anywhere,) * 3,
            scratch_shapes=[
                field,
                field,
                field,
                field,
                pltpu.VMEM(kernel.shape, BF16),
                pltpu.VMEM(left_factors.shape, BF16),
                pltpu.VMEM(right_factors.shape, BF16),
                pltpu.VMEM(kernel.shape, BF16),
                pltpu.VMEM((2, chunks, q, LANES), F32),
                field,
                field,
                pltpu.VMEM((q, LANES), F32),
                pltpu.VMEM((2, chunks, n_row * q, LANES), BF16),
                pltpu.VMEM((2, chunks, n_col, q, LANES), BF16),
                pltpu.VMEM((2, chunks, n_col, q, LANES), BF16),
                pltpu.VMEM((2, chunks, n_col, q, LANES), BF16),
                field,
                field,
                field,
                sem((4, chunks)),
                sem((3,)),
                sem((3, chunks)),
                sem((2, chunks, n_row - 1)),
                sem((2, chunks, n_row - 1)),
                sem((2, chunks, n_col)),
                sem((2, chunks, n_col)),
                sem((2, chunks, n_col)),
                sem((2, chunks, n_col)),
            ],
            compiler_params=pltpu.CompilerParams(
                collective_id=0, has_side_effects=True, vmem_limit_bytes=48 * 1024 * 1024
            ),
            cost_estimate=pl.CostEstimate(
                flops=4 * block * block * members,
                bytes_accessed=7 * 4 * q * members + 2 * block * block,
                transcendentals=8 * q * members,
            ),
        )(
            shear_stress,
            slip_state,
            friction_a,
            friction_b,
            kernel,
            left_factors,
            right_factors,
            admissible,
            ranks,
        )
    )


def solution(mesh):
    vector = P(("groups", "row", "col"), None)
    return jax.shard_map(
        functools.partial(per_device, mesh.shape["row"], mesh.shape["col"]),
        mesh=mesh,
        in_specs=(
            vector,
            vector,
            vector,
            vector,
            P(("groups", "row"), "col"),
            P(("groups", "row"), "col", None, None),
            P(("groups", "row"), "col", None, None),
            P(("groups", "row"), "col"),
            P(("groups", "row"), "col"),
        ),
        out_specs=(vector, vector, vector),
        check_vma=False,
    )
```

time: 125 us -> 64.1 us (0.51)
  waiting for transfers between devices: 87.4 us -> 0 us
  Pallas kernels: 0 us -> 53 us
  between operations: 13.8 us -> 0.66 us
  matrix products: 12.8 us -> 0 us
  other arithmetic: 8.85 us -> 0 us
  local copies, waits for them, and re-layouts: 2.16 us -> 9.8 us
    reduce_scatter x2 -> x0, waiting for transfers between devices: 54.5 us -> none  [friction_rates(): lax.psum_scatter(partial_value.astype(jnp.bfloat16), 'col', scatter_dimen...]
    pallas_call x0 -> x1, Pallas kernels: none -> 53 us  [per_device(): pl.pallas_call(functools.partial(step_kernel, n_row, n_col), out_shape=(o...]
    all_gather x2 -> x0, waiting for transfers between devices: 32.8 us -> none  [friction_rates(): gathered = lax.all_gather(deficit, 'row', axis=0, tiled=True)]
    dot_general x4 -> x0, matrix products: 12.8 us -> none  [the longest x2 8.94 us: friction_rates(): jnp.dot(kernel_tile, gathered, preferred_element_type=jnp.float32)]
    unnamed x17 -> x19, local copies, waits for them, and re-layouts: 1.55 us -> 9.8 us
    convert_element_type x3 -> x0, other arithmetic: 3.62 us -> none  [the longest x2 3.55 us: friction_rates(): deficit = (1.0 - speed_now).astype(jnp.bfloat16)]
    add x1 -> x0, other arithmetic: 3.14 us -> none  [per_device(): new_state = slip_state + 0.5 * time_step * (first_state + second_state)]
    mul x1 -> x0, other arithmetic: 2.08 us -> none  [per_device(): mean_rate = 0.5 * (first_stress + second_stress)]
  transfers between devices with their start and end apart: 4 -> 0, of which waited for: 4 -> 0; matrix products, arithmetic and copies ran while one was open for 2% -> 0% of each run, Pallas kernels for 0% -> 0%
where the time goes in v1:
time: 64.1 us; the launch traced here: 63.5 us
  Pallas kernels  53 us (83%)
  local copies, waits for them, and re-layouts  9.8 us (15%)
  between operations  0.66 us (1%)
    pallas_call x1, Pallas kernels, per_device(): pl.pallas_call(functools.partial(step_kernel, n_row, n_col), out_shape=(o...  53 us
    unnamed x19, local copies, waits for them, and re-layouts  9.8 us

profile of v1, /device:TPU:0, one launch (start us, length us, event | category | flops | bytes accessed | tf_op | source)
XLA Modules:
  0.0 63.5 jit_solution(17183555476391997895)
XLA Ops:
  0.6 0.0 copy-start
  0.6 1.0 %copy-done = f32[256,512]{1,0:T(8,128)S(1)} copy-done((f32[256,512]{1,0:T(8,128)S(1)}, f32[256,512]{1,0:T(8,128)}, u32[]{:S(2)}) %copy-start) | copy-done | bytes 524312
  1.7 0.0 copy-start.1
  1.7 1.0 %copy-done.1 = f32[256,512]{1,0:T(8,128)S(1)} copy-done((f32[256,512]{1,0:T(8,128)S(1)}, f32[256,512]{1,0:T(8,128)}, u32[]{:S(2)}) %copy-start.1) | copy-done | bytes 524312
  2.7 0.0 copy-start.2
  2.7 1.0 %copy-done.2 = f32[256,512]{1,0:T(8,128)S(1)} copy-done((f32[256,512]{1,0:T(8,128)S(1)}, f32[256,512]{1,0:T(8,128)}, u32[]{:S(2)}) %copy-start.2) | copy-done | bytes 524312
  3.8 0.0 copy-start.3
  3.8 1.0 %copy-done.3 = f32[256,512]{1,0:T(8,128)S(1)} copy-done((f32[256,512]{1,0:T(8,128)S(1)}, f32[256,512]{1,0:T(8,128)}, u32[]{:S(2)}) %copy-start.3) | copy-done | bytes 524312
  4.8 0.0 copy-start.4
  4.8 0.9 %copy-done.4 = bf16[4,4,32,256]{3,2,1,0:T(8,128)(2,1)S(1)} copy-done((bf16[4,4,32,256]{3,2,1,0:T(8,128)(2,1)S(1)}, bf16[4,4,32,256]{3,2,1,0:T(8,128)(2,1)}, u32[]{:S(2)}) %copy-start.4) | copy-done | bytes 262168
  5.8 0.0 copy-start.5
  5.8 0.9 %copy-done.5 = bf16[4,4,32,256]{3,2,1,0:T(8,128)(2,1)S(1)} copy-done((bf16[4,4,32,256]{3,2,1,0:T(8,128)(2,1)S(1)}, bf16[4,4,32,256]{3,2,1,0:T(8,128)(2,1)}, u32[]{:S(2)}) %copy-start.5) | copy-done | bytes 262168
  6.7 0.0 copy-start.6
  6.7 0.7 %copy-done.6 = s32[4,4]{1,0:T(4,128)S(1)} copy-done((s32[4,4]{1,0:T(4,128)S(1)}, s32[4,4]{1,0:T(4,128)}, u32[]{:S(2)}) %copy-start.6) | copy-done | bytes 88
  7.4 0.0 copy-start.7
  7.4 0.7 %copy-done.7 = s32[4,4]{1,0:T(4,128)S(1)} copy-done((s32[4,4]{1,0:T(4,128)S(1)}, s32[4,4]{1,0:T(4,128)}, u32[]{:S(2)}) %copy-start.7) | copy-done | bytes 88
  8.1 53.0 %shard_map.112 = (f32[256,512]{1,0:T(8,128)S(1)}, f32[256,512]{1,0:T(8,128)S(1)}, f32[256,512]{1,0:T(8,128)S(1)}) custom-call(f32[256,512]{1,0:T(8,128)S(1)} %copy-done, f32[256,512]{1,0:T(8,128)S(1)} %copy-done.1, f32[256,512]{1,0:T(8,128)S(1)} %copy-done.2, f32[256,512]{1,0:T(8,128)S(1)} %copy-done.3, bf16[1024,1024]{1,0:T(8,128)(2,1)} %kernel_hbm.1, ...), custom_call_target="tpu_custom_call" | custom-call | flops 2147483648 | bytes 5767168 | tf_op jit(solution)/shard_map/pallas_call | solution.py:329
  61.1 0.8 %copy.15 = f32[256,512]{1,0:T(8,128)} copy(f32[256,512]{1,0:T(8,128)S(1)} %get-tuple-element.6) | data formatting | bytes 1048576
  61.9 0.8 %copy.16 = f32[256,512]{1,0:T(8,128)} copy(f32[256,512]{1,0:T(8,128)S(1)} %get-tuple-element.7) | data formatting | bytes 1048576
  62.7 0.8 %copy.17 = f32[256,512]{1,0:T(8,128)} copy(f32[256,512]{1,0:T(8,128)S(1)} %get-tuple-element.8) | data formatting | bytes 1048576
Async XLA Ops:
  0.6 1.0 %copy-start = (f32[256,512]{1,0:T(8,128)S(1)}, f32[256,512]{1,0:T(8,128)}, u32[]{:S(2)}) copy-start(f32[256,512]{1,0:T(8,128)} %shear_hbm.1) | copy-start | bytes 1572868
  1.7 1.0 %copy-start.1 = (f32[256,512]{1,0:T(8,128)S(1)}, f32[256,512]{1,0:T(8,128)}, u32[]{:S(2)}) copy-start(f32[256,512]{1,0:T(8,128)} %slip_hbm.1) | copy-start | bytes 1572868
  2.7 1.0 %copy-start.2 = (f32[256,512]{1,0:T(8,128)S(1)}, f32[256,512]{1,0:T(8,128)}, u32[]{:S(2)}) copy-start(f32[256,512]{1,0:T(8,128)} %fa_hbm.1) | copy-start | bytes 1572868
  3.8 1.0 %copy-start.3 = (f32[256,512]{1,0:T(8,128)S(1)}, f32[256,512]{1,0:T(8,128)}, u32[]{:S(2)}) copy-start(f32[256,512]{1,0:T(8,128)} %fb_hbm.1) | copy-start | bytes 1572868
  4.8 0.9 %copy-start.4 = (bf16[4,4,32,256]{3,2,1,0:T(8,128)(2,1)S(1)}, bf16[4,4,32,256]{3,2,1,0:T(8,128)(2,1)}, u32[]{:S(2)}) copy-start(bf16[4,4,32,256]{3,2,1,0:T(8,128)(2,1)} %left_hbm.1) | copy-start | bytes 786436
  5.8 0.9 %copy-start.5 = (bf16[4,4,32,256]{3,2,1,0:T(8,128)(2,1)S(1)}, bf16[4,4,32,256]{3,2,1,0:T(8,128)(2,1)}, u32[]{:S(2)}) copy-start(bf16[4,4,32,256]{3,2,1,0:T(8,128)(2,1)} %right_hbm.1) | copy-start | bytes 786436
  6.7 0.7 %copy-start.6 = (s32[4,4]{1,0:T(4,128)S(1)}, s32[4,4]{1,0:T(4,128)}, u32[]{:S(2)}) copy-start(s32[4,4]{1,0:T(4,128)} %admissible.1) | copy-start | bytes 196
  7.4 0.7 %copy-start.7 = (s32[4,4]{1,0:T(4,128)S(1)}, s32[4,4]{1,0:T(4,128)}, u32[]{:S(2)}) copy-start(s32[4,4]{1,0:T(4,128)} %ranks.1) | copy-start | bytes 196

commit v2 on v1

--- a/solution.py
+++ b/solution.py
@@ -45,8 +45,8 @@
     total,
     slip_all,
     part,
-    from_low,
-    from_high,
+    relay,
+    inbox,
     out_stress,
     out_state,
     out_mean,
@@ -55,10 +55,10 @@
     out_sem,
     gather_send,
     gather_recv,
-    up_send,
-    up_recv,
-    down_send,
-    down_recv,
+    relay_send,
+    relay_recv,
+    inbox_send,
+    inbox_recv,
 ):
     row = lax.axis_index("row")
     col = lax.axis_index("col")
@@ -68,6 +68,9 @@
     sub = left.shape[3]
     rank_max = left.shape[2]
     lower_half = col < n_col // 2
+    at_end = (col == 0) | (col == n_col - 1)
+    beside_end = (col == 1) | (col == n_col - 2)
+    end = jnp.where(lower_half, 0, n_col - 1)
 
     def load(which, e):
         src = (shear_hbm, slip_hbm, fa_hbm, fb_hbm)[which]
@@ -87,13 +90,10 @@
             barrier, inc=1, device_id={"row": lax.rem(row + k, n_row)}, device_id_type=MESH
         )
 
-    @pl.when(col > 0)
-    def _():
-        pl.semaphore_signal(barrier, inc=1, device_id={"col": col - 1}, device_id_type=MESH)
-
-    @pl.when(col < n_col - 1)
-    def _():
-        pl.semaphore_signal(barrier, inc=1, device_id={"col": col + 1}, device_id_type=MESH)
+    for k in range(1, n_col):
+        pl.semaphore_signal(
+            barrier, inc=1, device_id={"col": lax.rem(col + k, n_col)}, device_id_type=MESH
+        )
 
     for e in range(chunks):
         for which in range(4):
@@ -124,23 +124,23 @@
         for k in range(1, n_row):
             gather_copy(sec, e, k).start()
 
-    def up_copy(sec, e, d):
+    def relay_copy(sec, e, d):
         return pltpu.make_async_remote_copy(
             src_ref=part.at[sec, e, d],
-            dst_ref=from_low.at[sec, e, d],
-            send_sem=up_send.at[sec, e, d],
-            recv_sem=up_recv.at[sec, e, d],
-            device_id={"col": col + 1},
+            dst_ref=relay.at[sec, e, d],
+            send_sem=relay_send.at[sec, e, d],
+            recv_sem=relay_recv.at[sec, e, d],
+            device_id={"col": jnp.where(lower_half, 1, n_col - 2)},
             device_id_type=MESH,
         )
 
-    def down_copy(sec, e, d):
+    def inbox_copy(sec, e, d, source):
         return pltpu.make_async_remote_copy(
             src_ref=part.at[sec, e, d],
-            dst_ref=from_high.at[sec, e, d],
-            send_sem=down_send.at[sec, e, d],
-            recv_sem=down_recv.at[sec, e, d],
-            device_id={"col": col - 1},
+            dst_ref=inbox.at[sec, e, source],
+            send_sem=inbox_send.at[sec, e, d],
+            recv_sem=inbox_recv.at[sec, e, source],
+            device_id={"col": d},
             device_id_type=MESH,
         )
 
@@ -151,8 +151,7 @@
         load(which, 0).wait()
     deficit_step(0, 0, s0[0], v0[0])
 
-    below, above = jnp.minimum(col, 1), jnp.minimum(n_col - 1 - col, 1)
-    pl.semaphore_wait(barrier, n_row - 1 + below + above)
+    pl.semaphore_wait(barrier, n_row - 1 + n_col - 1)
 
     start_gather(0, 0)
 
@@ -197,34 +196,26 @@
                 dense[rows, :], slips, preferred_element_type=F32
             ).astype(BF16)
 
-            @pl.when((col == 0) & (d > 0))
-            def _():
-                up_copy(sec, e, d).start()
-
-            @pl.when((col == n_col - 1) & (d < col))
-            def _():
-                down_copy(sec, e, d).start()
+            @pl.when(at_end & (d != col))
+            def _():
+                relay_copy(sec, e, d).start()
+
+            @pl.when((~at_end) & (d != col) & ((~beside_end) | (d == end)))
+            def _():
+                inbox_copy(sec, e, d, col).start()
 
     def forward(sec, e):
         @pl.loop(0, n_col)
         def _(i):
             d = target(i)
 
-            @pl.when((col > 0) & (d > col))
-            def _():
-                up_copy(sec, e, d).wait_recv()
+            @pl.when(beside_end & (d != col) & (d != end))
+            def _():
+                relay_copy(sec, e, d).wait_recv()
                 part[sec, e, d] = (
-                    part[sec, e, d].astype(F32) + from_low[sec, e, d].astype(F32)
+                    part[sec, e, d].astype(F32) + relay[sec, e, d].astype(F32)
                 ).astype(BF16)
-                up_copy(sec, e, d).start()
-
-            @pl.when((col < n_col - 1) & (d < col))
-            def _():
-                down_copy(sec, e, d).wait_recv()
-                part[sec, e, d] = (
-                    part[sec, e, d].astype(F32) + from_high[sec, e, d].astype(F32)
-                ).astype(BF16)
-                down_copy(sec, e, d).start()
+                inbox_copy(sec, e, d, col).start()
 
     def store(which, e):
         src = (out_stress, out_state, out_mean)[which]
@@ -236,15 +227,17 @@
     def finish(sec, e):
         total[...] = part[sec, e, col].astype(F32)
 
-        @pl.when(col > 0)
-        def _():
-            up_copy(sec, e, col).wait_recv()
-            total[...] += from_low[sec, e, col].astype(F32)
-
-        @pl.when(col < n_col - 1)
-        def _():
-            down_copy(sec, e, col).wait_recv()
-            total[...] += from_high[sec, e, col].astype(F32)
+        @pl.when(beside_end)
+        def _():
+            relay_copy(sec, e, col).wait_recv()
+            total[...] += relay[sec, e, col].astype(F32)
+
+        @pl.loop(1, n_col - 1)
+        def _(source):
+            @pl.when(source != col)
+            def _():
+                inbox_copy(sec, e, col, source).wait_recv()
+                total[...] += inbox[sec, e, source].astype(F32)
 
         @pl.when(sec == 0)
         def _():
@@ -290,13 +283,13 @@
 
         @pl.loop(0, n_col)
         def _(d):
-            @pl.when(d > col)
-            def _():
-                up_copy(sec, e, d).wait_send()
-
-            @pl.when(d < col)
-            def _():
-                down_copy(sec, e, d).wait_send()
+            @pl.when(at_end & (d != col))
+            def _():
+                relay_copy(sec, e, d).wait_send()
+
+            @pl.when((~at_end) & (d != col))
+            def _():
+                inbox_copy(sec, e, d, col).wait_send()
 
     @pl.loop(0, chunks)
     def _(e):
@@ -362,7 +355,7 @@
                 sem((2, chunks, n_col)),
             ],
             compiler_params=pltpu.CompilerParams(
-                collective_id=0, has_side_effects=True, vmem_limit_bytes=48 * 1024 * 1024
+                collective_id=0, has_side_effects=True, vmem_limit_bytes=62 * 1024 * 1024
             ),
             cost_estimate=pl.CostEstimate(
                 flops=4 * block * block * members,

time: 64.1 us -> 55.1 us (0.86)
  local copies, waits for them, and re-layouts: 9.8 us -> 4.59 us
  Pallas kernels: 53 us -> 49.7 us
    unnamed x19 -> x5, local copies, waits for them, and re-layouts: 9.8 us -> 4.59 us
    pallas_call x1, Pallas kernels: 53 us -> 49.7 us  [per_device(): pl.pallas_call(functools.partial(step_kernel, n_row, n_col), out_shape=(o...]
where the time goes in v2:
time: 55.1 us; the launch traced here: 54.9 us
  Pallas kernels  49.7 us (90%)
  local copies, waits for them, and re-layouts  4.59 us (8%)
  between operations  0.65 us (1%)
    pallas_call x1, Pallas kernels, per_device(): pl.pallas_call(functools.partial(step_kernel, n_row, n_col), out_shape=(o...  49.7 us
    unnamed x5, local copies, waits for them, and re-layouts  4.59 us

profile of v2, /device:TPU:0, one launch (start us, length us, event | category | flops | bytes accessed | tf_op | source)
XLA Modules:
  0.0 54.9 jit_solution(11082149900084890277)
XLA Ops:
  0.6 49.7 %shard_map.112 = (f32[256,512]{1,0:T(8,128)}, f32[256,512]{1,0:T(8,128)}, f32[256,512]{1,0:T(8,128)}) custom-call(f32[256,512]{1,0:T(8,128)} %shear_hbm.1, f32[256,512]{1,0:T(8,128)} %slip_hbm.1, f32[256,512]{1,0:T(8,128)} %fa_hbm.1, f32[256,512]{1,0:T(8,128)} %fb_hbm.1, bf16[1024,1024]{1,0:T(8,128)(2,1)} %kernel_hbm.1, bf16[4,4,32,256]{3,2,1,0:T(8,128)(2,1)} %left_hbm.1, ...), custom_call_target="tpu_custom_call" | custom-call | flops 2147483648 | bytes 5767168 | tf_op jit(solution)/shard_map/pallas_call | solution.py:322
  50.3 0.0 copy-start
  50.3 1.9 %copy.15 = f32[256,512]{1,0:T(8,128)} copy(f32[256,512]{1,0:T(8,128)} %get-tuple-element.6) | data formatting | bytes 1048576
  52.2 1.9 %copy.16 = f32[256,512]{1,0:T(8,128)} copy(f32[256,512]{1,0:T(8,128)} %get-tuple-element.7) | data formatting | bytes 1048576
  54.1 0.0 copy-done
  54.1 0.8 %copy.17 = f32[256,512]{1,0:T(8,128)} copy(f32[256,512]{1,0:T(8,128)S(1)} %copy-done) | data formatting | bytes 1048576
Async XLA Ops:
  50.3 3.8 %copy-start = (f32[256,512]{1,0:T(8,128)S(1)}, f32[256,512]{1,0:T(8,128)}, u32[]{:S(2)}) copy-start(f32[256,512]{1,0:T(8,128)} %get-tuple-element.8) | copy-start | bytes 1572868

commit v3 on v2

--- a/solution.py
+++ b/solution.py
@@ -30,7 +30,6 @@
     ranks,
     stress_hbm,
     state_hbm,
-    mean_hbm,
     s0,
     v0,
     fa,
@@ -49,7 +48,6 @@
     inbox,
     out_stress,
     out_state,
-    out_mean,
     in_sem,
     op_sem,
     out_sem,
@@ -218,8 +216,8 @@
                 inbox_copy(sec, e, d, col).start()
 
     def store(which, e):
-        src = (out_stress, out_state, out_mean)[which]
-        dst = (stress_hbm, state_hbm, mean_hbm)[which]
+        src = (out_stress, out_state)[which]
+        dst = (stress_hbm, state_hbm)[which]
         return pltpu.make_async_copy(
             src.at[e], dst.at[:, pl.ds(e * LANES, LANES)], out_sem.at[which, e]
         )
@@ -250,11 +248,9 @@
 
         @pl.when(sec == 1)
         def _():
-            mean = 0.5 * (first_stress[e] + total[...])
-            out_mean[e] = mean
-            out_stress[e] = s0[e] + time_step * mean
-            out_state[e] = v0[e] + 0.5 * time_step * (state_rate[0, e] + state_rate[1, e])
-            for which in range(3):
+            out_stress[e] = first_stress[e] + total[...]
+            out_state[e] = state_rate[0, e] + state_rate[1, e]
+            for which in range(2):
                 store(which, e).start()
 
     @pl.loop(0, steps + LAG_FINAL)
@@ -293,7 +289,7 @@
 
     @pl.loop(0, chunks)
     def _(e):
-        for which in range(3):
+        for which in range(2):
             store(which, e).wait()
 
 
@@ -318,12 +314,12 @@
     anywhere = pl.BlockSpec(memory_space=pl.ANY)
     scalars = pl.BlockSpec(memory_space=pltpu.SMEM)
     out = jax.ShapeDtypeStruct((q, members), F32)
-    return tuple(
+    stress_sum, state_sum = (
         pl.pallas_call(
             functools.partial(step_kernel, n_row, n_col),
-            out_shape=(out, out, out),
+            out_shape=(out, out),
             in_specs=[anywhere] * 7 + [scalars] * 2,
-            out_specs=(anywhere,) * 3,
+            out_specs=(anywhere,) * 2,
             scratch_shapes=[
                 field,
                 field,
@@ -343,10 +339,9 @@
                 pltpu.VMEM((2, chunks, n_col, q, LANES), BF16),
                 field,
                 field,
-                field,
                 sem((4, chunks)),
                 sem((3,)),
-                sem((3, chunks)),
+                sem((2, chunks)),
                 sem((2, chunks, n_row - 1)),
                 sem((2, chunks, n_row - 1)),
                 sem((2, chunks, n_col)),
@@ -374,6 +369,10 @@
             ranks,
         )
     )
+    mean_rate = 0.5 * stress_sum
+    new_stress = shear_stress + time_step * mean_rate
+    new_state = slip_state + 0.5 * time_step * state_sum
+    return new_stress, new_state, mean_rate
 
 
 def solution(mesh):

time: 55.1 us -> 53 us (0.962)
  local copies, waits for them, and re-layouts: 4.59 us -> 0.01 us
  other arithmetic: 0 us -> 2.46 us
    unnamed x5 -> x4, local copies, waits for them, and re-layouts: 4.59 us -> 0.01 us
    mul x0 -> x1, other arithmetic: none -> 2.46 us  [per_device(): mean_rate = 0.5 * stress_sum]
where the time goes in v3:
time: 53 us; the launch traced here: 52.8 us
  Pallas kernels  49.7 us (94%)
  other arithmetic  2.46 us (5%)
  between operations  0.67 us (1%)
    pallas_call x1, Pallas kernels, per_device(): pl.pallas_call(functools.partial(step_kernel, n_row, n_col), out_shape=(o...  49.7 us
    mul x1, other arithmetic, per_device(): mean_rate = 0.5 * stress_sum  2.46 us

profile of v3, /device:TPU:0, one launch (start us, length us, event | category | flops | bytes accessed | tf_op | source)
XLA Modules:
  0.0 52.8 jit_solution(5568521393132670905)
XLA Ops:
  0.6 0.0 copy-start.1
  0.6 0.0 copy-start
  0.7 49.7 %shard_map.112 = (f32[256,512]{1,0:T(8,128)}, f32[256,512]{1,0:T(8,128)}) custom-call(f32[256,512]{1,0:T(8,128)} %shear_hbm.1, f32[256,512]{1,0:T(8,128)} %slip_hbm.1, f32[256,512]{1,0:T(8,128)} %fa_hbm.1, f32[256,512]{1,0:T(8,128)} %fb_hbm.1, bf16[1024,1024]{1,0:T(8,128)(2,1)} %kernel_hbm.1, bf16[4,4,32,256]{3,2,1,0:T(8,128)(2,1)} %left_hbm.1, ...), custom_call_target="tpu_custom_call" | custom-call | flops 2147483648 | bytes 5767168 | tf_op jit(solution)/shard_map/pallas_call | solution.py:318
  50.3 0.0 copy-done.1
  50.3 0.0 copy-done
  50.4 2.5 %broadcast_multiply_fusion = (f32[256,512]{1,0:T(8,128)}, f32[256,512]{1,0:T(8,128)}, f32[256,512]{1,0:T(8,128)}) fusion(f32[256,512]{1,0:T(8,128)} %get-tuple-element.5, f32[256,512]{1,0:T(8,128)S(1)} %copy-done, f32[256,512]{1,0:T(8,128)S(1)} %copy-done.1, f32[256,512]{1,0:T(8,128)} %get-tuple-element.6), kind=kLoop, calls=%fused_computation.2 | loop fusion | flops 655360 | bytes 3670016 | tf_op jit(solution)/shard_map/mul | solution.py:372
Async XLA Ops:
  0.6 49.7 %copy-start.1 = (f32[256,512]{1,0:T(8,128)S(1)}, f32[256,512]{1,0:T(8,128)}, u32[]{:S(2)}) copy-start(f32[256,512]{1,0:T(8,128)} %slip_hbm.1) | copy-start | bytes 1572868
  0.6 49.7 %copy-start = (f32[256,512]{1,0:T(8,128)S(1)}, f32[256,512]{1,0:T(8,128)}, u32[]{:S(2)}) copy-start(f32[256,512]{1,0:T(8,128)} %shear_hbm.1) | copy-start | bytes 1572868
